TPU v7x, 32 devices: a whole 2x2x4 slice. The times are simulated.
32 devices in a mesh: seq: 8 (over z, y), batch: 4 (over x, core).
Axes of the slice: x: 2, y: 2, z: 4, core: 2. Of those that a mesh axis runs over, the one named last changes fastest.
Arguments:
- tokens: bfloat16 [4, 4096, 1536], P('batch', 'seq'), may hold values from -24 to 24
- filter_tap_weight: float32 [5, 1536], replicated, may hold values from -2.4 to 2.4
- norm_gain: float32 [1536], replicated, may hold values from 0.5 to 1.5
- query_weight: bfloat16 [1536, 512], replicated, may hold values from -4 to 4
- keyval_weight: bfloat16 [1536, 320], replicated, may hold values from -1 to 1
- head_weight: bfloat16 [768, 2, 384], replicated, may hold values from -0.21875 to 0.21875
- head_bias: float32 [2, 384], replicated, may hold values from -1 to 1
- exon_start: int32 [4, 32, 8], P('batch'), may hold values from 0 to 4095, as said below
- exon_end: int32 [4, 32, 8], P('batch'), may hold values from 0 to 4096, as said below
- gene_strand: int32 [4, 32], P('batch'), may hold values from 0 to 1
- gene_owner: int32 [4, 32, 1], P('batch'), may hold values from 0 to 3; in each aligned block of 32 rows (0 to 31, 32 to 63, ..., all dimensions but the last counted through in order) at most 16 rows name the same one
- gene_target: float32 [4, 4, 16, 384], P('batch'), may hold values from 0 to 4
Outputs:
- coverage: bfloat16 [4, 4096, 2, 384], P('batch', 'seq')
- gene_pred: float32 [4, 4, 16, 384], P('batch')
- head_grad: float32 [768, 2, 384], replicated
- bias_grad: float32 [2, 384], replicated
Inputs may be any that keep to these rules, and one draw needn't show every extreme that they name: `exon_start`: exons of a gene lie inside the window in increasing order without intersection, each of 1 to 4 bins; unused exon slots have start equal to end; every gene has at least one exon. `exon_end`: as exon_start. `gene_owner`: at most 16 genes of one window have the same owner.
All inputs are finite; a program needn't handle non-finite values.
Results may differ from a plain program's by a relative error of at most 0.025.
Values may be sent and summed in bfloat16 or wider, within the bound.
A program may use at most 64 MiB of HBM per device.

v0:
```python
import math

import jax
import jax.numpy as jnp
from jax import lax
from jax.sharding import PartitionSpec as P

HEADS = 4
DK = 128
DV = 192
TRK = 384
FILTER_TAP_COUNT = 5
DILATION_STRIDE = 64


def extended(block, sides, width):
    for axis, dim in sides:
        count = lax.axis_size(axis)
        forward = [(i, i + 1) for i in range(count - 1)]
        backward = [(target, source) for source, target in forward]
        low = lax.ppermute(
            lax.slice_in_dim(block, block.shape[dim] - width, None, axis=dim), axis, forward
        )
        high = lax.ppermute(lax.slice_in_dim(block, 0, width, axis=dim), axis, backward)
        block = jnp.concatenate([low, block, high], axis=dim)
    return block


def make_fold(query_rows, scale_factor, state_now, pieces):
    key_rows, value_rows = pieces
    key_count = key_rows.shape[0]
    block_rows = math.gcd(key_count, 512)
    block_count = key_count // block_rows
    key_blocks = key_rows.reshape(block_count, block_rows, key_rows.shape[1])
    value_blocks = value_rows.reshape(block_count, block_rows, value_rows.shape[1])

    def one_block(running, block_pair):
        running_max, running_sum, weighted = running
        key_block, value_block = block_pair
        scores = (
            jnp.einsum("qhd,kd->qhk", query_rows, key_block, preferred_element_type=jnp.float32)
            * scale_factor
        )
        new_max = jnp.maximum(running_max, jnp.max(scores, axis=-1))
        shrink = jnp.exp(running_max - new_max)
        weights = jnp.exp(scores - new_max[..., None])
        running_sum = running_sum * shrink + jnp.sum(weights, axis=-1)
        weighted = weighted * shrink[..., None] + jnp.einsum(
            "qhk,kd->qhd",
            weights.astype(jnp.bfloat16),
            value_block,
            preferred_element_type=jnp.float32,
        )
        return ((new_max, running_sum, weighted), None)

    result_state, unused = lax.scan(one_block, state_now, (key_blocks, value_blocks))
    return result_state


def local(
    tokens,
    filter_tap_weight,
    norm_gain,
    query_weight,
    keyval_weight,
    head_weight,
    head_bias,
    exon_start,
    exon_end,
    gene_strand,
    gene_owner,
    gene_target,
):
    local_rows = tokens[0]
    window_row_count = local_rows.shape[0]
    dilation_reach_rows = FILTER_TAP_COUNT // 2 * DILATION_STRIDE
    zero_extended = extended(local_rows, (("seq", 0),), dilation_reach_rows)
    tap_total = local_rows.astype(jnp.float32)
    for filter_tap_index in range(FILTER_TAP_COUNT):
        tap_total = tap_total + filter_tap_weight[filter_tap_index] * zero_extended[
            filter_tap_index * DILATION_STRIDE : filter_tap_index * DILATION_STRIDE
            + window_row_count
        ].astype(jnp.float32)
    spread = jnp.mean(tap_total * tap_total, axis=-1, keepdims=True)
    normed = (tap_total * lax.rsqrt(spread + 1e-06) * norm_gain).astype(jnp.bfloat16)
    queries = jnp.dot(normed, query_weight, preferred_element_type=jnp.float32).astype(jnp.bfloat16)
    keyval = jnp.dot(normed, keyval_weight, preferred_element_type=jnp.float32)
    key_rows = keyval[:, :DK].astype(jnp.bfloat16)
    value_rows = keyval[:, DK:].astype(jnp.bfloat16)
    query_rows = queries.reshape(window_row_count, HEADS, DK)
    start_state = (
        jnp.full((window_row_count, HEADS), -jnp.inf, jnp.float32),
        jnp.zeros((window_row_count, HEADS), jnp.float32),
        jnp.zeros((window_row_count, HEADS, DV), jnp.float32),
    )
    running_max, running_sum, weighted = make_fold(
        query_rows,
        DK ** (-0.5),
        start_state,
        (
            lax.all_gather(key_rows, "seq", axis=0, tiled=True),
            lax.all_gather(value_rows, "seq", axis=0, tiled=True),
        ),
    )
    hidden_width = HEADS * DV
    attended = (
        (weighted / running_sum[..., None])
        .reshape(window_row_count, hidden_width)
        .astype(jnp.bfloat16)
    )
    logits = jnp.dot(
        attended, head_weight.reshape(hidden_width, 2 * TRK), preferred_element_type=jnp.float32
    ) + head_bias.reshape(2 * TRK)
    coverage = jax.nn.softplus(logits).astype(jnp.bfloat16).reshape(1, window_row_count, 2, TRK)
    positions = lax.axis_index("seq") * window_row_count + jnp.arange(
        window_row_count, dtype=jnp.int32
    )
    starts = exon_start[0]
    exon_stops = exon_end[0]
    inside = (positions[None, None, :] >= starts[:, :, None]) & (
        positions[None, None, :] < exon_stops[:, :, None]
    )
    counts = jnp.sum(inside.astype(jnp.int32), axis=1).astype(jnp.bfloat16)
    partial_pool = jnp.dot(counts, attended, preferred_element_type=jnp.float32)
    pooled = lax.psum(partial_pool.astype(jnp.bfloat16), "seq").astype(jnp.float32)
    length = jnp.sum((exon_stops - starts).astype(jnp.float32), axis=1)
    pooled = pooled / length[:, None]
    track_share = TRK
    weight_part = head_weight.astype(jnp.float32)
    per_strand = (
        jnp.einsum("gh,hst->gst", pooled, weight_part, precision=lax.Precision.HIGHEST)
        + head_bias[None]
    )
    strands = gene_strand[0]
    gene_logit = jnp.where(strands[:, None] == 0, per_strand[:, 0], per_strand[:, 1])
    owners = gene_owner[0, :, 0]
    gene_index = jnp.arange(owners.shape[0], dtype=jnp.int32)
    earlier = (owners[:, None] == owners[None, :]) & (gene_index[None, :] < gene_index[:, None])
    slot_rank = jnp.sum(earlier.astype(jnp.int32), axis=1)
    capacity = gene_target.shape[2]
    owner_count = lax.axis_size("batch")
    slot_index = owners * capacity + slot_rank
    slot_table = (
        jnp.arange(owner_count * capacity, dtype=jnp.int32)[:, None] == slot_index[None, :]
    ).astype(jnp.float32)
    outgoing = jnp.dot(
        slot_table, jax.nn.softplus(gene_logit), precision=lax.Precision.HIGHEST
    ).reshape(owner_count, capacity, track_share)
    arrived = lax.all_to_all(
        outgoing.astype(jnp.bfloat16), "batch", split_axis=0, concat_axis=0, tiled=True
    ).astype(outgoing.dtype)
    target_part = gene_target[0]
    gene_slope = (jnp.log1p(arrived) - target_part) / (1.0 + arrived)
    returned = lax.all_to_all(
        gene_slope.astype(jnp.bfloat16), "batch", split_axis=0, concat_axis=0, tiled=True
    ).astype(gene_slope.dtype)
    slope_rows = jnp.dot(
        slot_table.T,
        returned.reshape(owner_count * capacity, track_share),
        precision=lax.Precision.HIGHEST,
    )
    logit_grad = slope_rows * jax.nn.sigmoid(gene_logit)
    placed = jnp.stack(
        [
            jnp.where(strands[:, None] == 0, logit_grad, 0.0),
            jnp.where(strands[:, None] == 1, logit_grad, 0.0),
        ],
        axis=1,
    )
    window_head = jnp.einsum("gh,gst->hst", pooled, placed, precision=lax.Precision.HIGHEST)
    window_bias = jnp.sum(placed, axis=0)
    head_grad, bias_grad = (
        lax.psum(window_head.astype(jnp.bfloat16), "batch").astype(jnp.float32),
        lax.psum(window_bias.astype(jnp.bfloat16), "batch").astype(jnp.float32),
    )
    return (coverage, arrived[None], head_grad, bias_grad)


def solution(mesh):
    in_specs = (
        P("batch", "seq", None),
        P(),
        P(),
        P(),
        P(),
        P(),
        P(),
        P("batch", None, None),
        P("batch", None, None),
        P("batch", None),
        P("batch", None, None),
        P("batch", None, None, None),
    )
    out_specs = (P("batch", "seq", None, None), P("batch", None, None, None), P(), P())
    return jax.shard_map(local, mesh=mesh, in_specs=in_specs, out_specs=out_specs, check_vma=False)
```

profile of v0, /device:TPU:0, one launch (start us, length us, event | category | flops | bytes accessed | tf_op | source)
XLA Modules:
  0.0 302.5 jit_solution(12533672885488948394)
XLA Ops:
  8.6 4.9 %collective-permute-start = (bf16[128,1536]{1,0:T(8,128)(2,1)S(1)}, bf16[128,1536]{1,0:T(8,128)(2,1)S(1)}, u32[]{:S(2)}, u32[]{:S(2)}) collective-permute-start(bf16[128,1536]{1,0:T(8,128)(2,1)S(1)} %get-tuple-element.115), channel_id=1, source_target_pairs={{0,4},{4,8},{8,12},{12,16},{16,20},{20,24},{24,28},{1,5},{5,9},{9,... | collective-permute-start | bytes 1179656 | tf_op jit(solution)/shard_map/ppermute | solution.py:21
  15.9 14.4 %collective-permute-done = bf16[128,1536]{1,0:T(8,128)(2,1)S(1)} collective-permute-done((bf16[128,1536]{1,0:T(8,128)(2,1)S(1)}, bf16[128,1536]{1,0:T(8,128)(2,1)S(1)}, u32[]{:S(2)}, u32[]{:S(2)}) %collective-permute-start) | collective-permute-done | bytes 393248 | tf_op jit(solution)/shard_map/ppermute | solution.py:21
  37.3 3.8 %convolution_convert_fusion.1 = bf16[512,512]{0,1:T(8,128)(2,1)} fusion(bf16[1536,512]{1,0:T(8,128)(2,1)S(1)} %copy-done, f32[512,1536]{1,0:T(8,128)} %copy-done.2, f32[1536]{0:T(1024)S(1)} %copy-done.17, f32[512]{0:T(512)S(1)} %add_rsqrt_fusion), kind=kOutput, calls=%fused_computation.43 | convolution fusion | flops 807927808 | bytes 5251072 | tf_op jit(solution)/shard_map/dot_general | solution.py:86
  43.1 33.4 %all-gather.3.cloned.1.call-done = bf16[4096,128]{0,1:T(8,128)(2,1)} async-done(((bf16[512,128]{0,1:T(8,128)(2,1)}), bf16[4096,128]{0,1:T(8,128)(2,1)}) %all-gather.3.cloned.1.call-update) | async-done | bytes 1048592 | tf_op jit(solution)/shard_map/all_gather | solution.py:101
  76.5 2.3 copy.33
  78.8 44.6 %all-gather.5.cloned.1.call-done = bf16[4096,192]{0,1:T(8,128)(2,1)} async-done(((bf16[512,192]{0,1:T(8,128)(2,1)}), bf16[4096,192]{0,1:T(8,128)(2,1)}) %all-gather.5.cloned.1.call-update) | async-done | bytes 1572880 | tf_op jit(solution)/shard_map/all_gather | solution.py:102
  123.3 2.7 copy.41
  126.0 75.7 %while.15 = (s32[]{:T(128)}, f32[512,4]{0,1:T(4,128)S(1)}, f32[512,4]{0,1:T(4,128)S(1)}, f32[512,4,192]{0,2,1:T(8,128)S(1)}, bf16[8,512,128]{2,1,0:T(8,128)(2,1)...) while((s32[]{:T(128)}, f32[512,4]{0,1:T(4,128)S(1)}, ...), condition=%wide.region_4.5_spmd.clone, body=%wide.region_1.4_spmd.clone.sunk | while | flops 680667136 | bytes 33490052 | solution.py:56
  126.0 3.7 %bitcast_reduce_fusion.2 = (f32[512,4]{0,1:T(4,128)S(1)}, f32[512,512,4]{1,0,2:T(8,128)}) fusion(bf16[512,4,128]{2,0,1:T(8,128)(2,1)} %get-tuple-element.195, bf16[8,512,128]{2,1,0:T(8,128)(2,1)} %get-tuple-element.194, s32[]{:T(128)} %get-tuple-element.181), kind=kOutput, calls=%fused_computation.1.clone.1 | convolution fusion | flops 270530560 | bytes 4858368 | tf_op jit(solution)/shard_map/while/body/eval_jaxpr/qhd,kd->qhk/dot_general | solution.py:41
  129.8 3.1 %fusion.81 = f32[512,4]{0,1:T(4,128)S(1)} fusion(f32[512,512,4]{1,0,2:T(8,128)} %get-tuple-element.169, f32[512,4]{0,1:T(4,128)S(1)} %select_maximum_fusion.2), kind=kLoop, calls=%fused_computation.4.clone.1 | loop fusion | flops 3143680 | bytes 4210688 | tf_op jit(solution)/shard_map/while/body/eval_jaxpr/reduce_sum | solution.py:47
  133.2 2.2 fusion.83
  135.5 3.8 %bitcast_reduce_fusion.2 = (f32[512,4]{0,1:T(4,128)S(1)}, f32[512,512,4]{1,0,2:T(8,128)}) fusion(bf16[512,4,128]{2,0,1:T(8,128)(2,1)} %get-tuple-element.195, bf16[8,512,128]{2,1,0:T(8,128)(2,1)} %get-tuple-element.194, s32[]{:T(128)} %get-tuple-element.181), kind=kOutput, calls=%fused_computation.1.clone.1 | convolution fusion | flops 270530560 | bytes 4858368 | tf_op jit(solution)/shard_map/while/body/eval_jaxpr/qhd,kd->qhk/dot_general | solution.py:41
  139.3 3.1 %fusion.81 = f32[512,4]{0,1:T(4,128)S(1)} fusion(f32[512,512,4]{1,0,2:T(8,128)} %get-tuple-element.169, f32[512,4]{0,1:T(4,128)S(1)} %select_maximum_fusion.2), kind=kLoop, calls=%fused_computation.4.clone.1 | loop fusion | flops 3143680 | bytes 4210688 | tf_op jit(solution)/shard_map/while/body/eval_jaxpr/reduce_sum | solution.py:47
  145.0 3.8 %bitcast_reduce_fusion.2 = (f32[512,4]{0,1:T(4,128)S(1)}, f32[512,512,4]{1,0,2:T(8,128)}) fusion(bf16[512,4,128]{2,0,1:T(8,128)(2,1)} %get-tuple-element.195, bf16[8,512,128]{2,1,0:T(8,128)(2,1)} %get-tuple-element.194, s32[]{:T(128)} %get-tuple-element.181), kind=kOutput, calls=%fused_computation.1.clone.1 | convolution fusion | flops 270530560 | bytes 4858368 | tf_op jit(solution)/shard_map/while/body/eval_jaxpr/qhd,kd->qhk/dot_general | solution.py:41
  148.7 3.1 %fusion.81 = f32[512,4]{0,1:T(4,128)S(1)} fusion(f32[512,512,4]{1,0,2:T(8,128)} %get-tuple-element.169, f32[512,4]{0,1:T(4,128)S(1)} %select_maximum_fusion.2), kind=kLoop, calls=%fused_computation.4.clone.1 | loop fusion | flops 3143680 | bytes 4210688 | tf_op jit(solution)/shard_map/while/body/eval_jaxpr/reduce_sum | solution.py:47
  154.4 3.8 %bitcast_reduce_fusion.2 = (f32[512,4]{0,1:T(4,128)S(1)}, f32[512,512,4]{1,0,2:T(8,128)}) fusion(bf16[512,4,128]{2,0,1:T(8,128)(2,1)} %get-tuple-element.195, bf16[8,512,128]{2,1,0:T(8,128)(2,1)} %get-tuple-element.194, s32[]{:T(128)} %get-tuple-element.181), kind=kOutput, calls=%fused_computation.1.clone.1 | convolution fusion | flops 270530560 | bytes 4858368 | tf_op jit(solution)/shard_map/while/body/eval_jaxpr/qhd,kd->qhk/dot_general | solution.py:41
  158.2 3.1 %fusion.81 = f32[512,4]{0,1:T(4,128)S(1)} fusion(f32[512,512,4]{1,0,2:T(8,128)} %get-tuple-element.169, f32[512,4]{0,1:T(4,128)S(1)} %select_maximum_fusion.2), kind=kLoop, calls=%fused_computation.4.clone.1 | loop fusion | flops 3143680 | bytes 4210688 | tf_op jit(solution)/shard_map/while/body/eval_jaxpr/reduce_sum | solution.py:47
  163.9 3.8 %bitcast_reduce_fusion.2 = (f32[512,4]{0,1:T(4,128)S(1)}, f32[512,512,4]{1,0,2:T(8,128)}) fusion(bf16[512,4,128]{2,0,1:T(8,128)(2,1)} %get-tuple-element.195, bf16[8,512,128]{2,1,0:T(8,128)(2,1)} %get-tuple-element.194, s32[]{:T(128)} %get-tuple-element.181), kind=kOutput, calls=%fused_computation.1.clone.1 | convolution fusion | flops 270530560 | bytes 4858368 | tf_op jit(solution)/shard_map/while/body/eval_jaxpr/qhd,kd->qhk/dot_general | solution.py:41
  167.6 3.1 %fusion.81 = f32[512,4]{0,1:T(4,128)S(1)} fusion(f32[512,512,4]{1,0,2:T(8,128)} %get-tuple-element.169, f32[512,4]{0,1:T(4,128)S(1)} %select_maximum_fusion.2), kind=kLoop, calls=%fused_computation.4.clone.1 | loop fusion | flops 3143680 | bytes 4210688 | tf_op jit(solution)/shard_map/while/body/eval_jaxpr/reduce_sum | solution.py:47
  173.3 3.8 %bitcast_reduce_fusion.2 = (f32[512,4]{0,1:T(4,128)S(1)}, f32[512,512,4]{1,0,2:T(8,128)}) fusion(bf16[512,4,128]{2,0,1:T(8,128)(2,1)} %get-tuple-element.195, bf16[8,512,128]{2,1,0:T(8,128)(2,1)} %get-tuple-element.194, s32[]{:T(128)} %get-tuple-element.181), kind=kOutput, calls=%fused_computation.1.clone.1 | convolution fusion | flops 270530560 | bytes 4858368 | tf_op jit(solution)/shard_map/while/body/eval_jaxpr/qhd,kd->qhk/dot_general | solution.py:41
  177.1 3.1 %fusion.81 = f32[512,4]{0,1:T(4,128)S(1)} fusion(f32[512,512,4]{1,0,2:T(8,128)} %get-tuple-element.169, f32[512,4]{0,1:T(4,128)S(1)} %select_maximum_fusion.2), kind=kLoop, calls=%fused_computation.4.clone.1 | loop fusion | flops 3143680 | bytes 4210688 | tf_op jit(solution)/shard_map/while/body/eval_jaxpr/reduce_sum | solution.py:47
  182.8 3.8 %bitcast_reduce_fusion.2 = (f32[512,4]{0,1:T(4,128)S(1)}, f32[512,512,4]{1,0,2:T(8,128)}) fusion(bf16[512,4,128]{2,0,1:T(8,128)(2,1)} %get-tuple-element.195, bf16[8,512,128]{2,1,0:T(8,128)(2,1)} %get-tuple-element.194, s32[]{:T(128)} %get-tuple-element.181), kind=kOutput, calls=%fused_computation.1.clone.1 | convolution fusion | flops 270530560 | bytes 4858368 | tf_op jit(solution)/shard_map/while/body/eval_jaxpr/qhd,kd->qhk/dot_general | solution.py:41
  186.6 3.1 %fusion.81 = f32[512,4]{0,1:T(4,128)S(1)} fusion(f32[512,512,4]{1,0,2:T(8,128)} %get-tuple-element.169, f32[512,4]{0,1:T(4,128)S(1)} %select_maximum_fusion.2), kind=kLoop, calls=%fused_computation.4.clone.1 | loop fusion | flops 3143680 | bytes 4210688 | tf_op jit(solution)/shard_map/while/body/eval_jaxpr/reduce_sum | solution.py:47
  192.3 3.8 %bitcast_reduce_fusion.2 = (f32[512,4]{0,1:T(4,128)S(1)}, f32[512,512,4]{1,0,2:T(8,128)}) fusion(bf16[512,4,128]{2,0,1:T(8,128)(2,1)} %get-tuple-element.195, bf16[8,512,128]{2,1,0:T(8,128)(2,1)} %get-tuple-element.194, s32[]{:T(128)} %get-tuple-element.181), kind=kOutput, calls=%fused_computation.1.clone.1 | convolution fusion | flops 270530560 | bytes 4858368 | tf_op jit(solution)/shard_map/while/body/eval_jaxpr/qhd,kd->qhk/dot_general | solution.py:41
  196.0 3.1 %fusion.81 = f32[512,4]{0,1:T(4,128)S(1)} fusion(f32[512,512,4]{1,0,2:T(8,128)} %get-tuple-element.169, f32[512,4]{0,1:T(4,128)S(1)} %select_maximum_fusion.2), kind=kLoop, calls=%fused_computation.4.clone.1 | loop fusion | flops 3143680 | bytes 4210688 | tf_op jit(solution)/shard_map/while/body/eval_jaxpr/reduce_sum | solution.py:47
  203.2 34.8 %psum.21 = bf16[32,768]{1,0:T(8,128)(2,1)S(1)} all-reduce(bf16[32,768]{1,0:T(8,128)(2,1)S(1)} %convolution_convert_fusion.4), channel_id=1, replica_groups=mesh['seq'=8,'batch'=4] {'seq'}, use_global_device_ids=true, to_apply=%region_7.8 | all-reduce | flops 24576 | bytes 98304 | tf_op jit(solution)/shard_map/psum | solution.py:125
  240.3 6.7 %all_to_all.10 = bf16[4,16,384]{2,1,0:T(8,128)(2,1)S(1)} all-to-all(bf16[4,16,384]{2,1,0:T(8,128)(2,1)S(1)} %convolution_convert_fusion.3), channel_id=1, replica_groups=mesh['seq'=8,'batch'=4] {'batch'}, dimensions={0} | all-to-all | bytes 98304 | tf_op jit(solution)/shard_map/all_to_all | solution.py:149
  247.7 6.4 %all_to_all.11 = bf16[4,16,384]{2,1,0:T(8,128)(2,1)S(1)} all-to-all(bf16[4,16,384]{2,1,0:T(8,128)(2,1)S(1)} %fusion.33), channel_id=1, replica_groups=mesh['seq'=8,'batch'=4] {'batch'}, dimensions={0} | all-to-all | bytes 98304 | tf_op jit(solution)/shard_map/all_to_all | solution.py:154
  254.9 3.1 %convolution_convert_fusion = bf16[768,2,384]{2,0,1:T(8,128)(2,1)} fusion(f32[32,1,384]{2,0,1:T(8,128)S(1)} %get-tuple-element.118, f32[32,1,384]{2,0,1:T(8,128)S(1)} %get-tuple-element.117, bf16[32,768]{1,0:T(8,128)(2,1)S(1)} %psum.21, f32[32]{0:T(128)S(1)} %convert_reduce_fusion.2), kind=kOutput, calls=%fused_computation.42 | convolution fusion | flops 227155968 | bytes 1327232 | tf_op jit(solution)/shard_map/gh,gst->hst/dot_general | solution.py:170
  262.4 6.3 %psum.23 = bf16[2,384]{1,0:T(2,128)(2,1)S(1)} all-reduce(bf16[2,384]{1,0:T(2,128)(2,1)S(1)} %fusion.36), channel_id=1, replica_groups=mesh['seq'=8,'batch'=4] {'batch'}, use_global_device_ids=true, to_apply=%region_11.12 | all-reduce | flops 768 | bytes 3072 | tf_op jit(solution)/shard_map/psum | solution.py:174
  269.3 22.7 %all-reduce.2.cloned.1.call-done = bf16[768,2,384]{2,0,1:T(8,128)(2,1)} async-done(((bf16[768,2,384]{2,0,1:T(8,128)(2,1)}), bf16[768,2,384]{2,0,1:T(8,128)(2,1)}) %all-reduce.2.cloned.1.call-update) | async-done | bytes 1179664 | tf_op jit(solution)/shard_map/psum | solution.py:173
  292.0 3.9 %copy.31 = f32[768,2,384]{2,1,0:T(2,128)} copy(bf16[768,2,384]{2,0,1:T(8,128)(2,1)} %all-reduce.2.cloned.1.call-done) | data formatting | bytes 3538944
  (132 shorter events, 41.5 us)
Async XLA Ops:
  7.2 30.1 %copy-start = (bf16[1536,512]{1,0:T(8,128)(2,1)S(1)}, bf16[1536,512]{1,0:T(8,128)(2,1)}, u32[]{:S(2)}) copy-start(bf16[1536,512]{1,0:T(8,128)(2,1)} %param.17) | copy-start | bytes 4718596
  7.2 23.0 %copy-start.3 = (bf16[1,512,1536]{2,1,0:T(8,128)(2,1)S(1)}, bf16[1,512,1536]{2,1,0:T(8,128)(2,1)}, u32[]{:S(2)}) copy-start(bf16[1,512,1536]{2,1,0:T(8,128)(2,1)} %param.14) | copy-start | bytes 4718596
  7.2 69.3 %all-gather.3.cloned.1.call-start = ((), (), s32[]{:S(2)}) async-start(), calls=%async_computation.2 | async-start | bytes 1179648 | tf_op jit(solution)/shard_map/all_gather | solution.py:101
  8.6 21.7 %collective-permute-start = (bf16[128,1536]{1,0:T(8,128)(2,1)S(1)}, bf16[128,1536]{1,0:T(8,128)(2,1)S(1)}, u32[]{:S(2)}, u32[]{:S(2)}) collective-permute-start(bf16[128,1536]{1,0:T(8,128)(2,1)S(1)} %get-tuple-element.115), channel_id=1, source_target_pairs={{0,4},{4,8},{8,12},{12,16},{16,20},{20,24},{24,28},{1,5},{5,9},{9,... | collective-permute-start | bytes 1179656 | tf_op jit(solution)/shard_map/ppermute | solution.py:21
  13.5 16.8 %collective-permute-start.1 = (bf16[128,1536]{1,0:T(8,128)(2,1)S(1)}, bf16[128,1536]{1,0:T(8,128)(2,1)S(1)}, u32[]{:S(2)}, u32[]{:S(2)}) collective-permute-start(bf16[128,1536]{1,0:T(8,128)(2,1)S(1)} %get-tuple-element.116), channel_id=1, source_target_pairs={{4,0},{8,4},{12,8},{16,12},{20,16},{24,20},{28,24},{5,1},{9,5},{13... | collective-permute-start | bytes 1179656 | tf_op jit(solution)/shard_map/ppermute | solution.py:24
  30.2 2.1 copy-start.7
  30.2 2.1 copy-start.17
  32.3 1.7 copy-start.2
  32.3 3.2 %copy-start.16 = (s32[1,32,8]{1,2,0:T(8,128)S(1)}, s32[1,32,8]{1,2,0:T(8,128)}, u32[]{:S(2)}) copy-start(s32[1,32,8]{1,2,0:T(8,128)} %param.21) | copy-start | bytes 3076
  32.4 3.2 %copy-start.15 = (s32[1,32,8]{1,2,0:T(8,128)S(1)}, s32[1,32,8]{1,2,0:T(8,128)}, u32[]{:S(2)}) copy-start(s32[1,32,8]{1,2,0:T(8,128)} %param.22) | copy-start | bytes 3076
  32.4 3.3 %copy-start.20 = (s32[1,32,1]{1,2,0:T(1,128)S(1)}, s32[1,32,1]{1,2,0:T(1,128)}, u32[]{:S(2)}) copy-start(s32[1,32,1]{1,2,0:T(1,128)} %param.24) | copy-start | bytes 388
  32.4 3.8 %copy-start.19 = (s32[1,32]{1,0:T(1,128)S(1)}, s32[1,32]{1,0:T(1,128)}, u32[]{:S(2)}) copy-start(s32[1,32]{1,0:T(1,128)} %param.23) | copy-start | bytes 388
  34.7 88.7 %all-gather.5.cloned.1.call-start = ((), (), s32[]{:S(2)}) async-start(), calls=%async_computation.3 | async-start | bytes 1769472 | tf_op jit(solution)/shard_map/all_gather | solution.py:102
  35.4 256.6 %all-reduce.2.cloned.1.call-start = ((), (), s32[]{:S(2)}) async-start(), calls=%async_computation.4 | async-start | bytes 2359296 | tf_op jit(solution)/shard_map/psum | solution.py:173
  129.8 3.4 %copy-start.1 = (f32[512,512,4]{1,0,2:T(8,128)S(1)}, f32[512,512,4]{1,0,2:T(8,128)}, u32[]{:S(2)}) copy-start(f32[512,512,4]{1,0,2:T(8,128)} %get-tuple-element.169) | copy-start | bytes 12582916 | tf_op jit(solution)/shard_map/while
  139.2 3.4 %copy-start.1 = (f32[512,512,4]{1,0,2:T(8,128)S(1)}, f32[512,512,4]{1,0,2:T(8,128)}, u32[]{:S(2)}) copy-start(f32[512,512,4]{1,0,2:T(8,128)} %get-tuple-element.169) | copy-start | bytes 12582916 | tf_op jit(solution)/shard_map/while
  148.7 3.4 %copy-start.1 = (f32[512,512,4]{1,0,2:T(8,128)S(1)}, f32[512,512,4]{1,0,2:T(8,128)}, u32[]{:S(2)}) copy-start(f32[512,512,4]{1,0,2:T(8,128)} %get-tuple-element.169) | copy-start | bytes 12582916 | tf_op jit(solution)/shard_map/while
  158.2 3.4 %copy-start.1 = (f32[512,512,4]{1,0,2:T(8,128)S(1)}, f32[512,512,4]{1,0,2:T(8,128)}, u32[]{:S(2)}) copy-start(f32[512,512,4]{1,0,2:T(8,128)} %get-tuple-element.169) | copy-start | bytes 12582916 | tf_op jit(solution)/shard_map/while
  167.6 3.4 %copy-start.1 = (f32[512,512,4]{1,0,2:T(8,128)S(1)}, f32[512,512,4]{1,0,2:T(8,128)}, u32[]{:S(2)}) copy-start(f32[512,512,4]{1,0,2:T(8,128)} %get-tuple-element.169) | copy-start | bytes 12582916 | tf_op jit(solution)/shard_map/while
  177.1 3.4 %copy-start.1 = (f32[512,512,4]{1,0,2:T(8,128)S(1)}, f32[512,512,4]{1,0,2:T(8,128)}, u32[]{:S(2)}) copy-start(f32[512,512,4]{1,0,2:T(8,128)} %get-tuple-element.169) | copy-start | bytes 12582916 | tf_op jit(solution)/shard_map/while
  186.6 3.4 %copy-start.1 = (f32[512,512,4]{1,0,2:T(8,128)S(1)}, f32[512,512,4]{1,0,2:T(8,128)}, u32[]{:S(2)}) copy-start(f32[512,512,4]{1,0,2:T(8,128)} %get-tuple-element.169) | copy-start | bytes 12582916 | tf_op jit(solution)/shard_map/while
  196.0 3.4 %copy-start.1 = (f32[512,512,4]{1,0,2:T(8,128)S(1)}, f32[512,512,4]{1,0,2:T(8,128)}, u32[]{:S(2)}) copy-start(f32[512,512,4]{1,0,2:T(8,128)} %get-tuple-element.169) | copy-start | bytes 12582916 | tf_op jit(solution)/shard_map/while
  201.7 36.2 %copy-start.18 = (f32[2,384]{1,0:T(2,128)S(1)}, f32[2,384]{1,0:T(2,128)}, u32[]{:S(2)}) copy-start(f32[2,384]{1,0:T(2,128)} %param.20) | copy-start | bytes 9220
  202.0 0.9 copy-start.4
  202.0 38.0 %copy-start.21 = (pred[32]{0:T(512)(128)(4,1)S(1)}, pred[32]{0:T(512)(128)(4,1)}, u32[]{:S(2)}) copy-start(pred[32]{0:T(512)(128)(4,1)} %get-tuple-element.120) | copy-start | bytes 100
  202.0 38.0 %copy-start.22 = (s32[32]{0:T(128)S(1)}, s32[32]{0:T(128)}, u32[]{:S(2)}) copy-start(s32[32]{0:T(128)} %multiply_add_fusion.1) | copy-start | bytes 388
  202.0 45.6 %copy-start.14 = (f32[1,4,16,384]{3,2,1,0:T(8,128)S(1)}, f32[1,4,16,384]{3,2,1,0:T(8,128)}, u32[]{:S(2)}) copy-start(f32[1,4,16,384]{3,2,1,0:T(8,128)} %param.25) | copy-start | bytes 294916
  240.0 18.1 %copy-start.6 = (bf16[768,2,384]{2,1,0:T(2,128)(2,1)S(1)}, bf16[768,2,384]{2,1,0:T(2,128)(2,1)}, u32[]{:S(2)}) copy-start(bf16[768,2,384]{2,1,0:T(2,128)(2,1)} %param.19) | copy-start | bytes 3538948
  258.0 1.1 copy-start.5
  259.2 2.5 copy-start.9
  259.2 3.2 %copy-start.11 = (f32[32,1,384]{2,0,1:T(8,128)S(1)}, f32[32,1,384]{2,0,1:T(8,128)}, u32[]{:S(2)}) copy-start(f32[32,1,384]{2,0,1:T(8,128)} %copy-done.10) | copy-start | bytes 147460
  259.2 3.2 %copy-start.13 = (f32[32,1,384]{2,0,1:T(8,128)S(1)}, f32[32,1,384]{2,0,1:T(8,128)}, u32[]{:S(2)}) copy-start(f32[32,1,384]{2,0,1:T(8,128)} %copy-done.12) | copy-start | bytes 147460
  (3 other events, 1.9 us)
Sparse Core Ops, SparseCore 0:
  34.8 41.6 all-gather.2
  79.1 44.1 all-gather.4
  258.2 33.8 all-reduce.1
where the time goes:
time: 303 us; the launch traced here: 302 us
  waiting for transfers between devices  115 us (38%)
  matrix products  59.8 us (20%)
  blocking collectives  54.2 us (18%)
  other arithmetic  29.8 us (10%)
  local copies, waits for them, and re-layouts  22.9 us (8%)
  between operations  14.1 us (5%)
  starting transfers between devices  6.31 us (2%)
    all_gather x1, waiting for transfers between devices, local(): lax.all_gather(value_rows, 'seq', axis=0, tiled=True)  44.6 us
    psum x1, blocking collectives, local(): lax.psum(partial_pool.astype(jnp.bfloat16), 'seq').astype(jnp.float32)  34.8 us
    all_gather x1, waiting for transfers between devices, local(): lax.all_gather(key_rows, 'seq', axis=0, tiled=True)  33.4 us
    dot_general x8, matrix products, one_block(): jnp.einsum('qhd,kd->qhk', query_rows, key_block, preferred_element_type=j...  30 us
    reduce_sum x8, other arithmetic, one_block(): running_sum = running_sum * shrink + jnp.sum(weights, axis=-1)  24.4 us
    psum x1, waiting for transfers between devices, local(): lax.psum(window_head.astype(jnp.bfloat16), 'batch').astype(jnp.float32)  22.7 us
    dot_general x8, matrix products, one_block(): jnp.einsum('qhk,kd->qhd', weights.astype(jnp.bfloat16), value_block, pref...  17.8 us
    ppermute x1, waiting for transfers between devices, extended(): lax.ppermute(lax.slice_in_dim(block, block.shape[dim] - width, None, axis...  14.4 us
  transfers between devices with their start and end apart: 5, of which 4 were waited for; matrix products, arithmetic and copies ran while one was open for 5% of the time, Pallas kernels for 0%

commit v1 on v0

v1 whole, which is shorter than its diff:
```python
import functools
import math

import jax
import jax.numpy as jnp
from jax import lax
from jax.experimental import pallas as pl
from jax.experimental.pallas import tpu as pltpu
from jax.sharding import PartitionSpec as P

HEADS = 4
DK = 128
DV = 192
TRK = 384
TAPS = 5
STRIDE = 64
REACH = TAPS // 2 * STRIDE
CHUNK = 128
MESH = pl.DeviceIdType.MESH
F32 = jnp.float32
BF16 = jnp.bfloat16
NT = (((1,), (1,)), ((), ()))


def softplus(x):
    return jnp.maximum(x, 0.0) + jnp.log1p(jnp.exp(-jnp.abs(x)))


def remote(src, dst, send_sem, recv_sem, device):
    return pltpu.make_async_remote_copy(
        src_ref=src,
        dst_ref=dst,
        send_sem=send_sem,
        recv_sem=recv_sem,
        device_id=device,
        device_id_type=MESH,
    )


def ring_place(s, n):
    odd = s % 2
    return (1 - odd) * (s // 2) + odd * (n - 1 - s // 2)


def ring_member(p, n):
    back = p // (n // 2)
    return (1 - back) * (2 * p) + back * (2 * (n - 1 - p) + 1)


def attention_kernel(
    n, tok, taps, gain, wq, wkv, out,
    ext, wq_v, wkv_v, q, kbuf, vbuf, m, l, acc,
    local_sem, halo_send, halo_recv, ring_send, ring_recv,
):
    rows = tok.shape[0]
    s = lax.axis_index("seq")
    p = ring_place(s, n)
    right = ring_member((p + 1) % n, n)
    left = ring_member((p + n - 1) % n, n)

    own = pltpu.make_async_copy(tok, ext.at[pl.ds(REACH, rows)], local_sem.at[0])
    own.start()
    get_kv = pltpu.make_async_copy(wkv, wkv_v, local_sem.at[1])
    get_kv.start()
    get_q = pltpu.make_async_copy(wq, wq_v, local_sem.at[2])
    get_q.start()

    barrier = pltpu.get_barrier_semaphore()
    has_low = s > 0
    has_high = s < n - 1
    for peer in (left, right):
        pl.semaphore_signal(barrier, inc=1, device_id={"seq": peer}, device_id_type=MESH)

    @pl.when(has_low)
    def _():
        pl.semaphore_signal(barrier, inc=1, device_id={"seq": s - 1}, device_id_type=MESH)

    @pl.when(has_high)
    def _():
        pl.semaphore_signal(barrier, inc=1, device_id={"seq": s + 1}, device_id_type=MESH)

    @pl.when(has_low & has_high)
    def _():
        pl.semaphore_wait(barrier, 4)

    @pl.when(jnp.logical_not(has_low & has_high))
    def _():
        pl.semaphore_wait(barrier, 3)

    to_high = remote(
        tok.at[pl.ds(rows - REACH, REACH)], ext.at[pl.ds(0, REACH)],
        halo_send.at[0], halo_recv.at[0], {"seq": (s + 1) % n},
    )
    to_low = remote(
        tok.at[pl.ds(0, REACH)], ext.at[pl.ds(REACH + rows, REACH)],
        halo_send.at[1], halo_recv.at[1], {"seq": (s + n - 1) % n},
    )

    @pl.when(has_high)
    def _():
        to_high.start()

    @pl.when(has_low)
    def _():
        to_low.start()

    @pl.when(jnp.logical_not(has_low))
    def _():
        ext[pl.ds(0, REACH), :] = jnp.zeros((REACH, ext.shape[1]), BF16)

    @pl.when(jnp.logical_not(has_high))
    def _():
        ext[pl.ds(REACH + rows, REACH), :] = jnp.zeros((REACH, ext.shape[1]), BF16)

    m[...] = jnp.full(m.shape, -1e30, F32)
    l[...] = jnp.zeros(l.shape, F32)
    acc[...] = jnp.zeros(acc.shape, F32)

    factor = DK ** (-0.5) * math.log2(math.e)

    def project(base, piece, offset):
        conv = ext[pl.ds(base + 2 * STRIDE, CHUNK), :].astype(F32)
        for k in range(TAPS):
            conv = conv + taps[pl.ds(k, 1), :] * ext[pl.ds(base + k * STRIDE, CHUNK), :].astype(F32)
        spread = jnp.mean(conv * conv, axis=-1, keepdims=True)
        normed = (conv * lax.rsqrt(spread + 1e-06) * gain[...]).astype(BF16)
        kv = jnp.dot(normed, wkv_v[...], preferred_element_type=F32)
        kbuf[p, piece, pl.ds(offset, CHUNK), :] = kv[:, :DK].astype(BF16)
        vbuf[p, piece, :, pl.ds(offset, CHUNK)] = kv[:, DK:].T.astype(BF16)
        qq = (jnp.dot(normed, wq_v[...], preferred_element_type=F32) * factor).astype(BF16)
        for h in range(HEADS):
            q[h, pl.ds(base, CHUNK), :] = qq[:, h * DK : (h + 1) * DK]

    half = n // 2

    def shard_copies(way, step, piece):
        if way == 0:
            origin, peer = (p + n - step) % n, right
        else:
            origin, peer = (p + step) % n, left
        return [
            remote(
                buf.at[origin, piece], buf.at[origin, piece],
                ring_send.at[way, step, piece, j], ring_recv.at[way, step, piece, j],
                {"seq": peer},
            )
            for j, buf in enumerate((kbuf, vbuf))
        ]

    def start(way, step, piece):
        for c in shard_copies(way, step, piece):
            c.start()

    def attend(slot):
        def pair(i, carry):
            heads = [2 * i + j for j in range(2)]
            keys = kbuf[slot].reshape(rows, DK)
            v0, v1 = vbuf[slot, 0], vbuf[slot, 1]
            old = [(q[h], m[h], l[h], acc[h]) for h in heads]
            new = []
            for qh, mo, lo, ao in old:
                st = lax.dot_general(keys, qh, NT, preferred_element_type=F32)
                mn = jnp.maximum(mo, jnp.max(st, axis=0, keepdims=True))
                w = jnp.exp2(st - mn)
                shrink = jnp.exp2(mo - mn)
                ln = lo * shrink + jnp.sum(w, axis=0, keepdims=True)
                wb = w.astype(BF16)
                an = (
                    ao * shrink
                    + jnp.dot(v0, wb[: rows // 2], preferred_element_type=F32)
                    + jnp.dot(v1, wb[rows // 2 :], preferred_element_type=F32)
                )
                new.append((mn, ln, an))
            for h, (mn, ln, an) in zip(heads, new):
                m[h] = mn
                l[h] = ln
                acc[h] = an
            return carry

        lax.fori_loop(0, HEADS // 2, pair, 0)

    own.wait()
    get_kv.wait()
    get_q.wait()

    def inner(i, carry):
        project(pl.multiple_of((i + 1) * CHUNK, CHUNK), 0, pl.multiple_of(i * CHUNK, CHUNK))
        return carry

    lax.fori_loop(0, 2, inner, 0)
    start(0, 0, 0)
    start(1, 0, 0)

    @pl.when(has_low)
    def _():
        to_high.wait_recv()

    @pl.when(has_high)
    def _():
        to_low.wait_recv()

    def outer(i, carry):
        project(pl.multiple_of(i * (rows - CHUNK), CHUNK), 1, pl.multiple_of(i * CHUNK, CHUNK))
        return carry

    lax.fori_loop(0, 2, outer, 0)
    start(0, 0, 1)
    start(1, 0, 1)
    attend(p)

    for step in range(half):
        last = step == half - 1
        ways_pieces = [(0, 0), (1, 0), (0, 1), (1, 1)] if not last else [(0, 0), (1, 1)]
        for way, piece in ways_pieces:
            for c in shard_copies(way, step, piece):
                c.wait_recv()
            nxt = step + 1
            if nxt < half - 1 or (nxt == half - 1 and (way, piece) in ((0, 0), (1, 1))):
                start(way, nxt, piece)
        if not last:
            attend((p + n - 1 - step) % n)
            attend((p + 1 + step) % n)
        else:
            attend((p + half) % n)

    for h in range(HEADS):
        out[pl.ds(h * DV, DV), :] = (acc[h] / l[h]).astype(BF16)

    @pl.when(has_high)
    def _():
        to_high.wait_send()

    @pl.when(has_low)
    def _():
        to_low.wait_send()

    for step in range(half):
        last = step == half - 1
        ways_pieces = [(0, 0), (1, 0), (0, 1), (1, 1)] if not last else [(0, 0), (1, 1)]
        for way, piece in ways_pieces:
            for c in shard_copies(way, step, piece):
                c.wait_send()


def head_kernel(
    n, nb, att, weight, bias, starts, stops, strand, owner, target,
    cov, pred_out, pool_out, placed_out, bias_out,
    tgt_all, meta_all, pool_all, round_send, round_recv,
    local_sem, tgt_send, tgt_recv, meta_send, meta_recv, pool_send, pool_recv, rs_send, rs_recv,
):
    rows = att.shape[1]
    genes = starts.shape[0]
    cap = target.shape[1]
    s = lax.axis_index("seq")
    b = lax.axis_index("batch")
    rounds = n.bit_length() - 1

    keep = pltpu.make_async_copy(target, tgt_all.at[b], local_sem.at[0])
    keep.start()
    barrier = pltpu.get_barrier_semaphore()
    partners = []
    for r in range(rounds):
        bit = 1 << r
        partners.append(s + bit - 2 * bit * ((s // bit) % 2))
    for partner in partners:
        pl.semaphore_signal(barrier, inc=1, device_id={"seq": partner}, device_id_type=MESH)
    for d in range(1, nb):
        pl.semaphore_signal(barrier, inc=1, device_id={"batch": (b + d) % nb}, device_id_type=MESH)

    lane = lax.broadcasted_iota(jnp.int32, (genes, 128), 1)
    meta_all[b] = jnp.where(lane == 0, strand[...], owner[...]).astype(F32)
    spot = s * rows + lax.broadcasted_iota(jnp.int32, (genes, rows), 1)
    counts = jnp.zeros((genes, rows), F32)
    length = jnp.zeros((genes, 1), F32)
    for e in range(starts.shape[1]):
        lo, hi = starts[:, e : e + 1], stops[:, e : e + 1]
        counts = counts + jnp.where((spot >= lo) & (spot < hi), 1.0, 0.0)
        length = length + (hi - lo).astype(F32)
    partial = lax.dot_general(counts.astype(BF16), att[...], NT, preferred_element_type=F32)

    pl.semaphore_wait(barrier, rounds + nb - 1)

    def coverage(i):
        block = att[:, i * CHUNK : (i + 1) * CHUNK].astype(F32).T.astype(BF16)
        logits = jnp.dot(block, weight[...], preferred_element_type=F32) + bias[...]
        cov[pl.ds(i * CHUNK, CHUNK), :] = softplus(logits).astype(BF16)

    todo = list(range(rows // CHUNK))
    early = []
    for r in range(rounds):
        round_send[r] = partial.astype(BF16)
        c = remote(
            round_send.at[r], round_recv.at[r], rs_send.at[r], rs_recv.at[r], {"seq": partners[r]}
        )
        c.start()
        if r == 0:
            for d in range(1, nb):
                peer = {"batch": (b + d) % nb}
                early.append(remote(target, tgt_all.at[b], tgt_send.at[d - 1], tgt_recv.at[d - 1], peer))
                early.append(
                    remote(meta_all.at[b], meta_all.at[b], meta_send.at[d - 1], meta_recv.at[d - 1], peer)
                )
            for e in early:
                e.start()
        if todo:
            coverage(todo.pop(0))
        c.wait()
        partial = round_send[r].astype(F32) + round_recv[r].astype(F32)

    pool_all[b] = (partial / length).astype(BF16)
    late = [
        remote(
            pool_all.at[b], pool_all.at[b], pool_send.at[d - 1], pool_recv.at[d - 1],
            {"batch": (b + d) % nb},
        )
        for d in range(1, nb)
    ]
    for c in late:
        c.start()
    while todo:
        coverage(todo.pop(0))
    keep.wait()
    for c in early:
        c.wait()
    for c in late:
        c.wait()

    pooled = pool_all[...].reshape(nb * genes, HEADS * DV)
    pool_out[...] = pooled
    both = jnp.dot(pooled, weight[...], preferred_element_type=F32) + bias[...]
    total = jnp.zeros((1, 2 * TRK), F32)
    gene_row = lax.broadcasted_iota(jnp.int32, (genes, genes), 0)
    gene_col = lax.broadcasted_iota(jnp.int32, (genes, genes), 1)
    slot_lane = lax.broadcasted_iota(jnp.int32, (genes, nb * cap), 1).astype(F32)
    lane_f = lane.astype(F32)
    for w in range(nb):
        strands = meta_all[w, :, 0:1]
        owners = meta_all[w, :, 1:2]
        hot = jnp.where(owners == lane_f, 1.0, 0.0).astype(BF16)
        same = lax.dot_general(hot, hot, NT, preferred_element_type=F32)
        rank = jnp.sum(jnp.where(gene_col < gene_row, same, 0.0), axis=1, keepdims=True)
        slot = owners * float(cap) + rank
        logit = both[w * genes : (w + 1) * genes]
        logit = jnp.where(strands == 0.0, logit[:, :TRK], logit[:, TRK:])
        pred = softplus(logit)
        table = jnp.where(slot == slot_lane, 1.0, 0.0)
        goals = tgt_all[:, w].reshape(nb * cap, TRK)
        goal = jnp.dot(table, goals, precision=lax.Precision.HIGHEST, preferred_element_type=F32)
        slope = (jnp.log1p(pred) - goal) / (1.0 + pred)
        grad = slope / (1.0 + jnp.exp(-logit))
        placed = jnp.concatenate(
            [jnp.where(strands == 0.0, grad, 0.0), jnp.where(strands == 0.0, 0.0, grad)], axis=1
        )
        placed_out[pl.ds(w * genes, genes), :] = placed.astype(BF16)
        total = total + jnp.sum(placed, axis=0, keepdims=True)
        mine = slot - (b * cap).astype(F32)
        pick = jnp.where((mine == lane_f) & (lane < cap), 1.0, 0.0).T
        records = jnp.dot(pick, pred, precision=lax.Precision.HIGHEST, preferred_element_type=F32)
        pred_out[w] = records[:cap]
    bias_out[...] = total


def local(
    n, nb, tokens, taps, gain, query_weight, keyval_weight, head_weight, head_bias,
    exon_start, exon_end, gene_strand, gene_owner, gene_target,
):
    rows, width = tokens.shape[1:]
    half = n // 2
    hidden = HEADS * DV
    vmem = pl.BlockSpec(memory_space=pltpu.VMEM)
    anywhere = pl.BlockSpec(memory_space=pl.ANY)
    dma = pltpu.SemaphoreType.DMA
    att = pl.pallas_call(
        functools.partial(attention_kernel, n),
        out_shape=jax.ShapeDtypeStruct((hidden, rows), BF16),
        in_specs=[anywhere, vmem, vmem, anywhere, anywhere],
        out_specs=vmem,
        scratch_shapes=[
            pltpu.VMEM((rows + 2 * REACH, width), BF16),
            pltpu.VMEM(query_weight.shape, BF16),
            pltpu.VMEM(keyval_weight.shape, BF16),
            pltpu.VMEM((HEADS, rows, DK), BF16),
            pltpu.VMEM((n, 2, rows // 2, DK), BF16),
            pltpu.VMEM((n, 2, DV, rows // 2), BF16),
            pltpu.VMEM((HEADS, 1, rows), F32),
            pltpu.VMEM((HEADS, 1, rows), F32),
            pltpu.VMEM((HEADS, DV, rows), F32),
            dma((3,)),
            dma((2,)),
            dma((2,)),
            dma((2, half, 2, 2)),
            dma((2, half, 2, 2)),
        ],
        compiler_params=pltpu.CompilerParams(
            collective_id=0, has_side_effects=True, vmem_limit_bytes=44 * 1024 * 1024
        ),
        name="attention",
    )(tokens[0], taps, gain.reshape(1, width), query_weight, keyval_weight)

    genes = exon_start.shape[1]
    cap = gene_target.shape[2]
    rounds = n.bit_length() - 1
    cov, pred, pooled, placed, bias_grad = pl.pallas_call(
        functools.partial(head_kernel, n, nb),
        out_shape=[
            jax.ShapeDtypeStruct((rows, 2 * TRK), BF16),
            jax.ShapeDtypeStruct((nb, cap, TRK), F32),
            jax.ShapeDtypeStruct((nb * genes, hidden), BF16),
            jax.ShapeDtypeStruct((nb * genes, 2 * TRK), BF16),
            jax.ShapeDtypeStruct((1, 2 * TRK), F32),
        ],
        in_specs=[vmem] * 8,
        out_specs=[vmem] * 5,
        scratch_shapes=[
            pltpu.VMEM((nb, nb, cap, TRK), F32),
            pltpu.VMEM((nb, genes, 128), F32),
            pltpu.VMEM((nb, genes, hidden), BF16),
            pltpu.VMEM((rounds, genes, hidden), BF16),
            pltpu.VMEM((rounds, genes, hidden), BF16),
            dma((1,)),
            dma((nb - 1,)),
            dma((nb - 1,)),
            dma((nb - 1,)),
            dma((nb - 1,)),
            dma((nb - 1,)),
            dma((nb - 1,)),
            dma((rounds,)),
            dma((rounds,)),
        ],
        compiler_params=pltpu.CompilerParams(
            collective_id=1, has_side_effects=True, vmem_limit_bytes=44 * 1024 * 1024
        ),
        name="heads",
    )(
        att,
        head_weight.reshape(hidden, 2 * TRK),
        head_bias.reshape(1, 2 * TRK),
        exon_start[0],
        exon_end[0],
        gene_strand.reshape(genes, 1),
        gene_owner[0],
        gene_target[0],
    )
    head_grad = jnp.einsum(
        "gh,gst->hst", pooled, placed.reshape(nb * genes, 2, TRK), preferred_element_type=F32
    )
    return (cov.reshape(1, rows, 2, TRK), pred[None], head_grad, bias_grad.reshape(2, TRK))


def solution(mesh):
    in_specs = (
        P("batch", "seq", None),
        P(),
        P(),
        P(),
        P(),
        P(),
        P(),
        P("batch", None, None),
        P("batch", None, None),
        P("batch", None),
        P("batch", None, None),
        P("batch", None, None, None),
    )
    out_specs = (P("batch", "seq", None, None), P("batch", None, None, None), P(), P())
    body = functools.partial(local, mesh.shape["seq"], mesh.shape["batch"])
    return jax.shard_map(body, mesh=mesh, in_specs=in_specs, out_specs=out_specs, check_vma=False)
```

time: 303 us -> 87.4 us (0.29)
  waiting for transfers between devices: 115 us -> 0 us
  Pallas kernels: 0 us -> 71.8 us
  matrix products: 59.8 us -> 0.49 us
  blocking collectives: 54.2 us -> 0 us
  other arithmetic: 29.8 us -> 0.01 us
  between operations: 14.1 us -> 0.73 us
  local copies, waits for them, and re-layouts: 22.9 us -> 14 us
  starting transfers between devices: 6.31 us -> 0 us
    all_gather x2 -> x0, waiting for transfers between devices: 77.9 us -> none  [the longest x1 44.6 us: local(): lax.all_gather(value_rows, 'seq', axis=0, tiled=True)]
    pallas_call x0 -> x2, Pallas kernels: none -> 71.8 us  [the longest x1 52.3 us: local(): pl.pallas_call(functools.partial(attention_kernel, n), out_shape=jax.Shap...]
    dot_general x24 -> x1, matrix products: 59.8 us -> 0.49 us  [local(): jnp.einsum('gh,gst->hst', pooled, placed.reshape(nb * genes, 2, TRK), pre...]
    psum x2 -> x0, blocking collectives: 41.1 us -> none  [the longest x1 34.8 us: local(): lax.psum(partial_pool.astype(jnp.bfloat16), 'seq').astype(jnp.float32)]
    reduce_sum x13 -> x0, other arithmetic: 27 us -> none  [the longest x8 24.4 us: one_block(): running_sum = running_sum * shrink + jnp.sum(weights, axis=-1)]
    psum x1 -> x0, waiting for transfers between devices: 22.7 us -> none  [local(): lax.psum(window_head.astype(jnp.bfloat16), 'batch').astype(jnp.float32)]
    ppermute x2 -> x0, waiting for transfers between devices: 14.4 us -> none  [the longest x1 14.4 us: extended(): lax.ppermute(lax.slice_in_dim(block, block.shape[dim] - width, None, axis...]
    all_to_all x2 -> x0, blocking collectives: 13.1 us -> none  [the longest x1 6.72 us: local(): lax.all_to_all(outgoing.astype(jnp.bfloat16), 'batch', split_axis=0, conc...]
  transfers between devices with their start and end apart: 5 -> 0, of which waited for: 4 -> 0; matrix products, arithmetic and copies ran while one was open for 5% -> 0% of each run, Pallas kernels for 0% -> 0%
where the time goes in v1:
time: 87.4 us; the launch traced here: 87.1 us
  Pallas kernels  71.8 us (82%)
  local copies, waits for them, and re-layouts  14 us (16%)
    pallas_call x1, Pallas kernels, local(): pl.pallas_call(functools.partial(attention_kernel, n), out_shape=jax.Shap...  52.3 us
    pallas_call x1, Pallas kernels, local(): pl.pallas_call(functools.partial(head_kernel, n, nb), out_shape=[jax.Shap...  19.5 us
    unnamed x17, local copies, waits for them, and re-layouts  10.2 us

profile of v1, /device:TPU:0, one launch (start us, length us, event | category | flops | bytes accessed | tf_op | source)
XLA Modules:
  0.0 87.1 jit_solution(12360627283209616121)
XLA Ops:
  0.6 0.0 copy-start.3
  0.6 0.0 copy-start
  0.7 0.8 copy.28
  1.5 0.7 reshape.29.gain
  2.2 0.8 copy.17
  2.9 0.8 copy.18
  3.7 0.7 copy.19.strand
  4.4 0.7 copy.20.owner
  5.2 1.7 %copy.16.wkv = bf16[1536,320]{1,0:T(8,128)(2,1)S(1)} copy(bf16[1536,320]{0,1:T(8,128)(2,1)} %param.16) | data formatting | bytes 1966080 | tf_op args[4]
  6.9 0.0 copy-done.3
  6.9 0.0 copy-done
  6.9 0.0 copy-start.1
  6.9 1.4 %copy-done.1 = bf16[1536,512]{1,0:T(8,128)(2,1)S(1)} copy-done((bf16[1536,512]{1,0:T(8,128)(2,1)S(1)}, bf16[1536,512]{1,0:T(8,128)(2,1)}, u32[]{:S(2)}) %copy-start.1) | copy-done | bytes 1572888
  8.3 0.0 copy-start.4
  8.3 52.3 %attention.1.att = bf16[768,512]{1,0:T(8,128)(2,1)S(1)} custom-call(bf16[512,1536]{1,0:T(8,128)(2,1)S(1)} %bitcast.20, f32[5,1536]{1,0:T(8,128)S(1)} %copy-done.3, f32[1,1536]{1,0:T(1,128)S(1)} %reshape.29.gain, bf16[1536,512]{1,0:T(8,128)(2,1)S(1)} %copy-done.1, bf16[1536,320]{1,0:T(8,128)(2,1)S(1)} %copy.16.wkv), custom_call_target="tpu_custom_call" | custom-call | tf_op jit(solution)/shard_map/attention/pallas_call | solution.py:373
  60.6 0.0 copy-done.4
  60.6 0.0 copy-start.2
  60.7 0.2 copy.27
  60.9 0.6 copy-done.2
  61.5 19.5 %heads.1 = (bf16[512,768]{1,0:T(8,128)(2,1)S(1)}, f32[4,16,384]{2,1,0:T(8,128)S(1)}, bf16[128,768]{1,0:T(8,128)(2,1)S(1)}, bf16[128,768]{1,0:T(8,128)(2,1)S(1)}, f32[1,768]{1,0:T(1,128)S(1)}) custom-call(bf16[768,512]{1,0:T(8,128)(2,1)S(1)} %attention.1.att, bf16[768,768]{1,0:T(8,128)(2,1)S(1)} %bitcast.19, f32[1,768]{1,0:T(1,128)S(1)} %bitcast.26, ...), custom_call_target="tpu_custom_call" | custom-call | tf_op jit(solution)/shard_map/heads/pallas_call | solution.py:403
  81.1 1.1 %reshape.33 = bf16[1,512,2,384]{3,2,1,0:T(2,128)(2,1)} reshape(bf16[512,768]{1,0:T(8,128)(2,1)S(1)} %get-tuple-element.9) | data formatting | bytes 1572864 | tf_op jit(solution)/shard_map/reshape | solution.py:447
  82.1 0.6 reshape.35
  82.7 0.5 fusion
  83.2 3.2 %copy.23 = f32[768,2,384]{2,1,0:T(2,128)} copy(f32[768,2,384]{2,0,1:T(8,128)S(1)} %fusion) | data formatting | bytes 4718592
  86.4 0.6 copy.34
  (1 shorter events, 0.0 us)
Async XLA Ops:
  0.6 6.2 %copy-start.3 = (f32[5,1536]{1,0:T(8,128)S(1)}, f32[5,1536]{1,0:T(8,128)}, u32[]{:S(2)}) copy-start(f32[5,1536]{1,0:T(8,128)} %taps.1) | copy-start | bytes 92164
  0.6 6.2 %copy-start = (bf16[1,512,1536]{2,1,0:T(8,128)(2,1)S(1)}, bf16[1,512,1536]{2,1,0:T(8,128)(2,1)}, u32[]{:S(2)}) copy-start(bf16[1,512,1536]{2,1,0:T(8,128)(2,1)} %param.12) | copy-start | bytes 4718596
  6.9 1.4 %copy-start.1 = (bf16[1536,512]{1,0:T(8,128)(2,1)S(1)}, bf16[1536,512]{1,0:T(8,128)(2,1)}, u32[]{:S(2)}) copy-start(bf16[1536,512]{1,0:T(8,128)(2,1)} %wq.1) | copy-start | bytes 4718596
  8.3 52.4 %copy-start.4 = (bf16[768,2,384]{2,1,0:T(2,128)(2,1)S(1)}, bf16[768,2,384]{2,1,0:T(2,128)(2,1)}, u32[]{:S(2)}) copy-start(bf16[768,2,384]{2,1,0:T(2,128)(2,1)} %param.17) | copy-start | bytes 3538948
  60.6 0.9 %copy-start.2 = (f32[1,4,16,384]{3,2,1,0:T(8,128)S(1)}, f32[1,4,16,384]{3,2,1,0:T(8,128)}, u32[]{:S(2)}) copy-start(f32[1,4,16,384]{3,2,1,0:T(8,128)} %param.23) | copy-start | bytes 294916
